TPU v7x, 128 devices: a whole 4x4x4 slice. The times are simulated.
128 devices in a mesh: chan: 16 (over y_lo, z, core), freq: 8 (over x, y_hi).
Axes of the slice: x: 4, y: 4 (y_hi: 2, y_lo: 2; y = y_hi * 2 + y_lo), z: 4, core: 2. Of those that a mesh axis runs over, the one named last changes fastest.
Arguments:
- records: bfloat16 [18432, 5120], P(('chan', 'freq')), may hold values from -6 to 6
- offsets: int32 [8], replicated, may hold values from 0 to 14336, as said below
- sources: int32 [64], replicated, may hold values from 0 to 5119
Outputs:
- cross_spectra: bfloat16 [2, 64, 5120, 2048], P(None, None, 'chan', 'freq')
Inputs may be any that keep to these rules, and one draw needn't show every extreme that they name: offsets never fall; the first is 0 and the last is 14336.
All inputs are finite; a program needn't handle non-finite values.
Results may differ from a plain program's by a relative error of at most 0.0068.
Values may be sent and summed in bfloat16 or wider, within the bound.
No kernel may reach another device: no remote copies, remote signals or barrier semaphores. Data moves between devices by JAX's collectives and lax.ppermute only.
A program may use at most 320 MiB of HBM per device.

v0:
```python
import jax
import jax.numpy as jnp
from jax import lax
from jax.sharding import PartitionSpec as P

NF = 2048
SEG = 8
HW = 32


EPSILON = 1e-06


def taper_window(length):
    steps = jnp.arange(length, dtype=jnp.int32).astype(jnp.float32)
    return 0.5 - 0.5 * jnp.cos(2.0 * jnp.pi * steps / length)


def fourier_table(freqs):
    length = 2 * freqs
    times = jnp.arange(length, dtype=jnp.int32)
    bins = jnp.arange(freqs, dtype=jnp.int32)
    angle = (times[:, None] * bins[None, :] % length).astype(jnp.float32) * (2.0 * jnp.pi / length)
    return jnp.concatenate([jnp.cos(angle), -jnp.sin(angle)], axis=1).astype(jnp.bfloat16)


def band_matrix(freqs, half):
    rows = jnp.arange(freqs, dtype=jnp.int32)
    inside = jnp.abs(rows[:, None] - rows[None, :]) <= half
    return (inside.astype(jnp.bfloat16), jnp.sum(inside.astype(jnp.float32), axis=0))


def whiten(spectrum, band, counts):
    real_part = spectrum[..., :NF]
    imag_part = spectrum[..., NF:]
    magnitude = jnp.sqrt(real_part * real_part + imag_part * imag_part).astype(jnp.bfloat16)
    smooth = jnp.einsum("scg,gf->scf", magnitude, band, preferred_element_type=jnp.float32)
    divisor = smooth / counts + EPSILON
    return jnp.stack([real_part / divisor, imag_part / divisor], axis=-2).astype(jnp.bfloat16)


def shards(records, offsets, sources):
    length = 2 * NF
    chan_count = lax.axis_size("chan")
    freq_count = lax.axis_size("freq")
    devices_all = chan_count * freq_count
    local_rows = records.shape[0]
    channels_all = records.shape[1]
    block_width = channels_all // devices_all
    window = taper_window(length)
    table = fourier_table(NF)
    band, counts = band_matrix(NF, HW)
    blocks = records.reshape(local_rows, devices_all, block_width)
    received = lax.all_to_all(blocks, ("chan", "freq"), split_axis=1, concat_axis=0, tiled=True)[
        :, 0, :
    ]
    pieces = [
        lax.dynamic_slice_in_dim(received, offsets[segment], length, 0) for segment in range(SEG)
    ]
    stacked = jnp.stack(pieces)
    tapered = (stacked.astype(jnp.float32) * window[None, :, None]).astype(jnp.bfloat16)
    spectrum = jnp.einsum("stc,tf->scf", tapered, table, preferred_element_type=jnp.float32)
    whitened = whiten(spectrum, band, counts)
    band_white = lax.all_to_all(whitened, "freq", split_axis=3, concat_axis=1, tiled=True)
    chan_width = band_white.shape[1]
    first_channel = lax.axis_index("chan") * chan_width
    columns = first_channel + jnp.arange(chan_width, dtype=jnp.int32)
    selector = (sources[:, None] == columns[None, :]).astype(jnp.bfloat16)
    picked = jnp.einsum("sj,kjpf->kspf", selector, band_white, preferred_element_type=jnp.float32)
    source_spectra = lax.psum(picked.astype(jnp.bfloat16), "chan").astype(jnp.float32)
    source_real = source_spectra[:, :, 0]
    source_imag = source_spectra[:, :, 1]
    white_real = band_white[:, :, 0].astype(jnp.float32)
    white_imag = band_white[:, :, 1].astype(jnp.float32)
    real_sum = jnp.einsum("ksf,krf->srf", source_real, white_real) + jnp.einsum(
        "ksf,krf->srf", source_imag, white_imag
    )
    imag_sum = jnp.einsum("ksf,krf->srf", source_real, white_imag) - jnp.einsum(
        "ksf,krf->srf", source_imag, white_real
    )
    return (jnp.stack([real_sum, imag_sum]) * (1.0 / SEG)).astype(jnp.bfloat16)


def solution(mesh):
    in_specs = (P(("chan", "freq"), None), P(), P())
    out_specs = P(None, None, "chan", "freq")
    return jax.shard_map(shards, mesh=mesh, in_specs=in_specs, out_specs=out_specs, check_vma=False)
```

profile of v0, /device:TPU:0, one launch (start us, length us, event | category | flops | bytes accessed | tf_op | source)
XLA Modules:
  0.0 625.7 jit_solution(14212814959073448611)
XLA Ops:
  6.5 3.9 copy.39
  10.4 11.1 %all-to-all-start = ((bf16[144,128,40]{0,2,1:T(8,128)(2,1)}), bf16[144,128,40]{0,2,1:T(8,128)(2,1)S(1)}, u32[]{:S(2)}, u32[]{:S(2)}) async-start(bf16[144,128,40]{0,2,1:T(8,128)(2,1)} %bitcast.89), calls=%async_computation | async-start | bytes 5242880 | tf_op jit(solution)/shard_map/all_to_all | solution.py:54
  21.6 135.6 %negate_convert_fusion = (bf16[4096,2048]{1,0:T(8,128)(2,1)}, bf16[4096,2048]{1,0:T(8,128)(2,1)}) fusion(), kind=kLoop, calls=%fused_computation.9 | loop fusion | flops 142606336 | bytes 33554432 | tf_op jit(solution)/shard_map/convert.5
  175.5 5.5 squeeze.39
  182.3 15.6 %fusion.6 = f32[8,40,4096]{2,1,0:T(8,128)S(1)} fusion(bf16[4096,2048]{1,0:T(8,128)(2,1)} %get-tuple-element.19, bf16[4096,2048]{1,0:T(8,128)(2,1)} %get-tuple-element.20, bf16[8,4096,40]{1,2,0:T(8,128)(2,1)S(1)} %bitcast_dynamic-update-slice_fusion, f32[4096]{0:T(1024)S(1)} %multiply_subtract_fusion), kind=kOutput, calls=%fused_computation.13 | convolution fusion | flops 10808459264 | bytes 41435136 | tf_op jit(solution)/shard_map/stc,tf->scf/dot_general | solution.py:62
  201.6 8.6 %copy.41 = bf16[8,40,2,2048]{1,0,2,3:T(8,128)(2,1)} copy(bf16[8,40,2,2048]{3,1,0,2:T(8,128)(2,1)S(1)} %pad_maximum_fusion) | data formatting | bytes 5242880 | tf_op jit(solution)/shard_map/stack | solution.py:39
  210.2 14.6 %reshape.22 = bf16[8,2,81920]{2,1,0:T(2,128)(2,1)} reshape(bf16[2048,2,8,40]{3,2,1,0:T(8,128)(2,1)} %bitcast.84) | data formatting | bytes 5242880
  224.8 6.2 all-to-all-start.1
  231.2 38.5 %all-to-all-done.1 = bf16[8,2,81920]{2,1,0:T(2,128)(2,1)S(1)} async-done(((bf16[8,2,81920]{2,1,0:T(2,128)(2,1)}), bf16[8,2,81920]{2,1,0:T(2,128)(2,1)S(1)}, u32[]{:S(2)}, u32[]{:S(2)}) %all-to-all-start.1) | async-done | bytes 2621472 | tf_op jit(solution)/shard_map/all_to_all | solution.py:64
  269.7 14.2 %reshape.23 = bf16[2048,2,8,40]{3,2,1,0:T(8,128)(2,1)} reshape(bf16[8,2,81920]{2,1,0:T(2,128)(2,1)S(1)} %all-to-all-done.1) | data formatting | bytes 5242880
  283.9 8.3 %copy.42 = bf16[8,40,2,8,256]{4,1,3,2,0:T(8,128)(2,1)S(1)} copy(bf16[8,40,2,8,256]{1,0,2,4,3:T(8,128)(2,1)} %bitcast.85) | data formatting | bytes 5242880 | tf_op jit(solution)/shard_map/all_to_all | solution.py:64
  299.7 111.0 %all-reduce.2.cloned.1.call-done = bf16[8,64,2,256]{3,1,2,0:T(8,128)(2,1)} async-done(((bf16[8,64,2,256]{3,1,2,0:T(8,128)(2,1)}), bf16[8,64,2,256]{3,1,2,0:T(8,128)(2,1)}) %all-reduce.2.cloned.1.call-update) | async-done | bytes 524304 | tf_op jit(solution)/shard_map/psum | solution.py:70
  415.6 12.8 %fusion.26 = f32[256,320,64]{1,2,0:T(8,128)} fusion(bf16[8,320,256]{1,0,2:T(8,128)(2,1)S(1)} %copy.43, bf16[8,64,256]{1,0,2:T(8,128)(2,1)} %copy.44), kind=kOutput, calls=%fused_computation.54 | convolution fusion | flops 83886080 | bytes 22544384 | tf_op jit(solution)/shard_map/ksf,krf->srf/dot_general | solution.py:75
  428.4 10.0 %fusion.29 = f32[256,320,64]{1,2,0:T(8,128)} fusion(bf16[8,320,256]{1,0,2:T(8,128)(2,1)S(1)} %copy.43, bf16[8,64,256]{1,0,2:T(8,128)(2,1)S(1)} %copy-done.2), kind=kOutput, calls=%fused_computation.57 | convolution fusion | flops 83886080 | bytes 22544384 | tf_op jit(solution)/shard_map/ksf,krf->srf/dot_general | solution.py:78
  438.5 10.1 %fusion.27 = f32[256,320,64]{1,2,0:T(8,128)} fusion(bf16[8,320,256]{1,0,2:T(8,128)(2,1)S(1)} %copy.45, bf16[8,64,256]{1,0,2:T(8,128)(2,1)S(1)} %copy-done.2), kind=kOutput, calls=%fused_computation.55 | convolution fusion | flops 83886080 | bytes 22544384 | tf_op jit(solution)/shard_map/ksf,krf->srf/dot_general | solution.py:75
  448.6 10.0 %fusion.28 = f32[256,320,64]{1,2,0:T(8,128)} fusion(bf16[8,320,256]{1,0,2:T(8,128)(2,1)S(1)} %copy.45, bf16[8,64,256]{1,0,2:T(8,128)(2,1)S(1)} %copy-done.1), kind=kOutput, calls=%fused_computation.56 | convolution fusion | flops 83886080 | bytes 22544384 | tf_op jit(solution)/shard_map/ksf,krf->srf/dot_general | solution.py:78
  458.7 23.3 %copy.47 = f32[256,320,64]{0,1,2:T(8,128)} copy(f32[256,320,64]{1,2,0:T(8,128)} %fusion.26) | data formatting | bytes 41943040 | tf_op jit(solution)/shard_map/ksf,krf->srf/dot_general | solution.py:75
  482.0 23.3 %copy.48 = f32[256,320,64]{0,1,2:T(8,128)} copy(f32[256,320,64]{1,2,0:T(8,128)} %fusion.27) | data formatting | bytes 41943040 | tf_op jit(solution)/shard_map/ksf,krf->srf/dot_general | solution.py:75
  505.3 23.3 %copy.54 = f32[256,320,64]{0,1,2:T(8,128)} copy(f32[256,320,64]{1,2,0:T(8,128)} %fusion.29) | data formatting | bytes 41943040 | tf_op jit(solution)/shard_map/ksf,krf->srf/dot_general | solution.py:78
  528.6 23.3 %copy.53 = f32[256,320,64]{0,1,2:T(8,128)} copy(f32[256,320,64]{1,2,0:T(8,128)} %fusion.28) | data formatting | bytes 41943040 | tf_op jit(solution)/shard_map/ksf,krf->srf/dot_general | solution.py:78
  551.9 22.6 %add_bitcast_fusion = f32[1,64,320,256]{3,2,1,0:T(8,128)} fusion(f32[256,320,64]{0,1,2:T(8,128)} %copy.47, f32[256,320,64]{0,1,2:T(8,128)} %copy.48), kind=kLoop, calls=%fused_computation.16 | loop fusion | flops 5242880 | bytes 62914560 | tf_op jit(solution)/shard_map/stack | solution.py:81
  574.5 4.0 copy-done
  578.5 17.2 %subtract_bitcast_fusion = f32[1,64,320,256]{3,2,1,0:T(8,128)} fusion(f32[256,320,64]{0,1,2:T(8,128)} %copy.53, f32[256,320,64]{0,1,2:T(8,128)S(1)} %copy-done), kind=kLoop, calls=%fused_computation.15 | loop fusion | flops 5242880 | bytes 62914560 | tf_op jit(solution)/shard_map/stack | solution.py:81
  595.7 23.1 %fusion = bf16[2,64,320,256]{3,2,1,0:T(8,128)(2,1)} fusion(f32[1,64,320,256]{3,2,1,0:T(8,128)} %subtract_bitcast_fusion, f32[1,64,320,256]{3,2,1,0:T(8,128)} %add_bitcast_fusion), kind=kLoop, calls=%fused_computation.4 | loop fusion | flops 31457280 | bytes 62914560 | tf_op jit(solution)/shard_map/convert_element_type | solution.py:81
  (34 shorter events, 21.0 us)
Async XLA Ops:
  10.4 163.0 %all-to-all-start = ((bf16[144,128,40]{0,2,1:T(8,128)(2,1)}), bf16[144,128,40]{0,2,1:T(8,128)(2,1)S(1)}, u32[]{:S(2)}, u32[]{:S(2)}) async-start(bf16[144,128,40]{0,2,1:T(8,128)(2,1)} %bitcast.89), calls=%async_computation | async-start | bytes 5242880 | tf_op jit(solution)/shard_map/all_to_all | solution.py:54
  21.6 135.6 %copy-start.3 = (s32[8]{0:T(128)S(1)}, s32[8]{0:T(128)}, u32[]{:S(2)}) copy-start(s32[8]{0:T(128)} %param.4) | copy-start | bytes 100
  224.8 44.9 %all-to-all-start.1 = ((bf16[8,2,81920]{2,1,0:T(2,128)(2,1)}), bf16[8,2,81920]{2,1,0:T(2,128)(2,1)S(1)}, u32[]{:S(2)}, u32[]{:S(2)}) async-start(bf16[8,2,81920]{2,1,0:T(2,128)(2,1)} %reshape.22), calls=%async_computation.1 | async-start | bytes 5242880 | tf_op jit(solution)/shard_map/all_to_all | solution.py:64
  230.9 179.7 %all-reduce.2.cloned.1.call-start = ((), (), s32[]{:S(2)}) async-start(), calls=%async_computation.2 | async-start | bytes 1048576 | tf_op jit(solution)/shard_map/psum | solution.py:70
  283.9 8.3 %copy-start.4 = (s32[64]{0:T(128)S(1)}, s32[64]{0:T(128)}, u32[]{:S(2)}) copy-start(s32[64]{0:T(128)} %param.5) | copy-start | bytes 772
  415.6 12.9 %copy-start.2 = (bf16[8,64,256]{1,0,2:T(8,128)(2,1)S(1)}, bf16[8,64,256]{1,0,2:T(8,128)(2,1)}, u32[]{:S(2)}) copy-start(bf16[8,64,256]{1,0,2:T(8,128)(2,1)} %copy.46) | copy-start | bytes 786436
  438.5 10.1 %copy-start.1 = (bf16[8,64,256]{1,0,2:T(8,128)(2,1)S(1)}, bf16[8,64,256]{1,0,2:T(8,128)(2,1)}, u32[]{:S(2)}) copy-start(bf16[8,64,256]{1,0,2:T(8,128)(2,1)} %copy.44) | copy-start | bytes 786436
  551.9 26.6 %copy-start = (f32[256,320,64]{0,1,2:T(8,128)S(1)}, f32[256,320,64]{0,1,2:T(8,128)}, u32[]{:S(2)}) copy-start(f32[256,320,64]{0,1,2:T(8,128)} %copy.54) | copy-start | bytes 62914564
Sparse Core Ops, SparseCore 0:
  293.8 116.8 all-reduce.1
where the time goes:
time: 628 us; the launch traced here: 626 us
  other arithmetic  199 us (32%)
  local copies, waits for them, and re-layouts  167 us (27%)
  waiting for transfers between devices  150 us (24%)
  matrix products  63.6 us (10%)
  between operations  28.4 us (5%)
  starting transfers between devices  17.6 us (3%)
    another operation x1, other arithmetic  136 us
    psum x1, waiting for transfers between devices, shards(): lax.psum(picked.astype(jnp.bfloat16), 'chan').astype(jnp.float32)  111 us
    another operation x2, other arithmetic, shards(): return (jnp.stack([real_sum, imag_sum]) * (1.0 / SEG)).astype(jnp.bfloat16)  39.8 us
    all_to_all x1, waiting for transfers between devices, shards(): lax.all_to_all(whitened, 'freq', split_axis=3, concat_axis=1, tiled=True)  38.5 us
    unnamed x20, local copies, waits for them, and re-layouts  37.8 us
    dot_general x1, local copies, waits for them, and re-layouts, shards(): jnp.einsum('ksf,krf->srf', source_imag, white_imag)  23.3 us
    dot_general x1, local copies, waits for them, and re-layouts, shards(): jnp.einsum('ksf,krf->srf', source_real, white_real)  23.3 us
    dot_general x1, local copies, waits for them, and re-layouts, shards(): jnp.einsum('ksf,krf->srf', source_imag, white_real)  23.3 us
  transfers between devices with their start and end apart: 3, of which 2 were waited for; matrix products, arithmetic and copies ran while one was open for 23% of the time, Pallas kernels for 0%

commit v1 on v0

v1 whole, which is shorter than its diff:
```python
import numpy as np
import jax
import jax.numpy as jnp
import ml_dtypes
from jax import lax
from jax.experimental import pallas as pl
from jax.experimental.pallas import tpu as pltpu
from jax.sharding import PartitionSpec as P

NF = 2048
LENGTH = 2 * NF
SEG = 8
NSRC = 64
HW = 32
EPSILON = 1e-06

DEVICES = 128
ROWS = 144
OWN = 40
PICKED = 8
CHANS = OWN + PICKED
LANES = SEG * CHANS
BANDS = 8
WIDTH = 256
THIRD = ROWS // 3
VMEM = 56 * 1024 * 1024

NT = (((1,), (1,)), ((), ()))


def step_tables():
    a = np.arange(256)
    first = np.zeros((256, 256))
    for g in range(16):
        for i in range(8):
            f1 = 8 * g + i
            first[16 * g + i] = np.cos(2 * np.pi * ((a * f1) % 256) / 256)
            first[16 * g + 8 + i] = -np.sin(2 * np.pi * ((a * f1) % 256) / 256)
    first[8] = np.cos(np.pi * a)
    b = np.arange(16)
    second = np.zeros((16, 256, 256))
    for g in range(16):
        for band in range(BANDS):
            for j in range(16):
                if j < 8:
                    low = 8 * g + j
                elif g == 0:
                    low = 128 if j == 15 else 249 + j - 8
                else:
                    low = 249 - 8 * g + j - 8
                f = 256 * band + low
                angle = 2 * np.pi * ((b * f) % 4096) / 4096
                c, s = np.cos(angle), np.sin(angle)
                if low <= 128:
                    sign, slot = 1.0, low - 8 * g
                else:
                    sign, slot = -1.0, 256 - low - 8 * g
                row = (band * 2) * 16 + j
                if low == 0:
                    second[g, row, 16 * b] = c
                    second[g, row + 16, 16 * b] = -s
                elif low == 128:
                    second[g, row, 16 * b + 8] = c
                    second[g, row + 16, 16 * b + 8] = -s
                else:
                    second[g, row, 16 * b + slot] = c
                    second[g, row, 16 * b + 8 + slot] = sign * s
                    second[g, row + 16, 16 * b + slot] = -s
                    second[g, row + 16, 16 * b + 8 + slot] = sign * c
    return first.astype(ml_dtypes.bfloat16), second.astype(ml_dtypes.bfloat16)


def window_tables():
    a = np.arange(256) * (2 * np.pi / 256)
    b = np.arange(16) * (2 * np.pi / 4096)
    rows = np.stack([np.cos(a), np.sin(a)])[:, :, None] * np.ones((1, 1, 128))
    return rows.astype(np.float32), np.stack([np.cos(b), np.sin(b)]).astype(np.float32)


def band_block():
    rows = np.arange(128)[:, None] + 64
    return (np.abs(rows - np.arange(256)[None, :]) <= HW).astype(ml_dtypes.bfloat16)


def lane(shape):
    return lax.broadcasted_iota(jnp.int32, shape, 1)


def pack_kernel(sources_ref, records_ref, out_ref, head_ref, tail_ref):
    picked = jnp.zeros((ROWS, 128), jnp.float32)
    for i in range(8):
        cols = lane((128, 640)) + 640 * i
        hot = (cols == sources_ref[...]).astype(jnp.bfloat16)
        picked += lax.dot_general(records_ref[:, 640 * i:640 * i + 640], hot, NT, preferred_element_type=jnp.float32)
    at8 = lane((8, 128))
    for band in range(BANDS):
        head_ref[band] = pltpu.roll(picked[:THIRD], (120 - 8 * band) % 128, 1)
        tail = jnp.zeros((8, 128), jnp.float32)
        for m in range(12):
            piece = pltpu.roll(picked[THIRD + 8 * m:THIRD + 8 * m + 8], (8 * m - 8 * band) % 128, 1)
            tail = jnp.where((at8 >= 8 * m) & (at8 < 8 * m + 8), piece, tail)
        tail_ref[band] = tail
    at = lane((THIRD, 128))

    def group(i, carry):
        for j in range(16):
            tile, start = divmod(OWN * j, 128)
            parts = []
            for u in range(3):
                shift = (OWN * u - start) % 128

                def piece(t):
                    base = pl.multiple_of(640 * i + 128 * t, 128)
                    x = records_ref[THIRD * u:THIRD * u + THIRD, pl.ds(base, 128)].astype(jnp.float32)
                    return pltpu.roll(x, shift, 1) if shift else x
                part = piece(tile)
                if start + OWN > 128:
                    part = jnp.where(at >= OWN * u + 128 - start, piece(tile + 1), part)
                parts.append(part)
            main = jnp.where(at < 40, parts[0], jnp.where(at < 80, parts[1], jnp.where(at < 120, parts[2], head_ref[j % 8])))
            out_ref[16 * i + j] = jnp.concatenate([main, tail_ref[j % 8]], axis=0).astype(jnp.bfloat16)
        return carry
    lax.fori_loop(0, 8, group, 0)


def spectrum_kernel(offsets_ref, fine_ref, got_ref, first_ref, second_ref, band_ref, coarse_ref, out_ref,
                    time_ref, x_ref, y_ref, spec_ref, mag_ref):
    own48 = lane((THIRD, 128)) < OWN

    def unpack(src, carry):
        block = got_ref[src].astype(jnp.float32)
        main, tail = block[:THIRD], block[THIRD:]
        by48 = pltpu.roll(main, 48, 1)
        by88 = pltpu.roll(main, 88, 1)
        tails = [pltpu.roll(tail, (OWN - 8 * m) % 128, 1) for m in range(12)]
        base = pl.multiple_of(src * ROWS, 8)
        time_ref[pl.ds(base, THIRD)] = jnp.where(own48, main, by48)
        time_ref[pl.ds(base + THIRD, THIRD)] = jnp.where(own48, by88, jnp.concatenate(tails[:6], axis=0))
        time_ref[pl.ds(base + 2 * THIRD, THIRD)] = jnp.where(own48, by48, jnp.concatenate(tails[6:], axis=0))
        return carry
    lax.fori_loop(0, DEVICES, unpack, 0)

    at = lane((64, 128))

    def residue(b, carry):
        cb, sb = fine_ref[0, b], fine_ref[1, b]
        for chunk in range(4):
            rows = slice(64 * chunk, 64 * chunk + 64)
            window = 0.5 - 0.5 * (coarse_ref[0, rows] * cb - coarse_ref[1, rows] * sb)
            placed = []
            for k in range(SEG):
                start = offsets_ref[k] + b + 1024 * chunk
                piece = time_ref[pl.ds(start, 64, 16)] * window
                shift = (CHANS * k) % 128
                placed.append(pltpu.roll(piece, shift, 1) if shift else piece)
            t0 = jnp.where(at < 48, placed[0], jnp.where(at < 96, placed[1], placed[2]))
            t1 = jnp.where(at < 16, placed[2], jnp.where(at < 64, placed[3], jnp.where(at < 112, placed[4], placed[5])))
            t2 = jnp.where(at < 32, placed[5], jnp.where(at < 80, placed[6], placed[7]))
            x_ref[rows] = jnp.concatenate([t0, t1, t2], axis=1).astype(jnp.bfloat16)
        y = jnp.dot(first_ref[...], x_ref[...], preferred_element_type=jnp.float32).astype(jnp.bfloat16)
        base = pl.multiple_of(16 * b, 16)
        for g in range(16):
            y_ref[g, pl.ds(base, 16)] = y[16 * g:16 * g + 16]
        return carry
    lax.fori_loop(0, 16, residue, 0)

    for g in range(16):
        z = jnp.dot(second_ref[g], y_ref[g], preferred_element_type=jnp.float32)
        for band in range(BANDS):
            for p in range(2):
                r = (band * 2 + p) * 16
                base = 256 * band
                spec_ref[p, base + 8 * g:base + 8 * g + 8] = z[r:r + 8]
                if g == 0:
                    spec_ref[p, base + 249:base + 256] = z[r + 8:r + 15]
                    spec_ref[p, base + 128:base + 129] = z[r + 15:r + 16]
                else:
                    spec_ref[p, base + 249 - 8 * g:base + 257 - 8 * g] = z[r + 8:r + 16]

    mag_ref[0:64] = jnp.zeros((64, LANES), jnp.bfloat16)
    mag_ref[64 + NF:128 + NF] = jnp.zeros((64, LANES), jnp.bfloat16)

    def magnitude(i, carry):
        rows = pl.ds(pl.multiple_of(i * 64, 64), 64)
        re, im = spec_ref[0, rows], spec_ref[1, rows]
        mag_ref[pl.ds(pl.multiple_of(i * 64 + 64, 64), 64)] = jnp.sqrt(re * re + im * im).astype(jnp.bfloat16)
        return carry
    lax.fori_loop(0, NF // 64, magnitude, 0)

    def whiten(band, carry):
        for half in range(2):
            base = pl.multiple_of(band * 256 + 128 * half, 128)
            total = jnp.dot(band_ref[...], mag_ref[pl.ds(base, 256)], preferred_element_type=jnp.float32)
            f = base + lax.broadcasted_iota(jnp.int32, (128, LANES), 0)
            count = (jnp.minimum(f + HW, NF - 1) - jnp.maximum(f - HW, 0) + 1).astype(jnp.float32)
            scale = count / (total + EPSILON * count)
            for p in range(2):
                white = spec_ref[p, pl.ds(base, 128)] * scale
                for t in range(3):
                    turned = jnp.transpose(white[:, 128 * t:128 * t + 128])
                    out_ref[band, p, 128 * t:128 * t + 128, 128 * half:128 * half + 128] = turned.astype(jnp.bfloat16)
        return carry
    lax.fori_loop(0, BANDS, whiten, 0)


def diagonals(arrays, at):
    for bit in (1, 2, 4):
        odd = ((at // 16) & bit) != 0
        arrays = [jnp.where(odd, arrays[(i + bit) % 8], arrays[i]) for i in range(8)]
    return arrays


def cross_kernel(got_ref, out_ref, wide_ref, left_ref, picked_ref, weight_ref, prod_ref):
    step = pl.program_id(0)
    chans = BANDS * OWN

    @pl.when(step == 0)
    def _():
        at = lane((CHANS, 128))

        def gather(src, carry):
            for p in range(2):
                for h in range(2):
                    cols = slice(128 * h, 128 * h + 128)
                    arrays = []
                    for k in range(SEG):
                        x = got_ref[src, p, CHANS * k:CHANS * k + CHANS, cols].astype(jnp.float32)
                        arrays.append(pltpu.roll(x, 16 * k, 1) if k else x)
                    arrays = diagonals(arrays, at)
                    for g in range(8):
                        x = arrays[-g % 8]
                        wide_ref[8 * h + g, pl.ds(pl.multiple_of(OWN * src, 8), OWN), 128 * p:128 * p + 128] = x[:OWN]
                        picked_ref[8 * h + g, pl.ds(pl.multiple_of(PICKED * src, 8), PICKED), 128 * p:128 * p + 128] = x[OWN:] * (1.0 / SEG)
            return carry
        lax.fori_loop(0, BANDS, gather, 0)

        def narrow(g, carry):
            left_ref[g] = wide_ref[g].astype(jnp.bfloat16)
            return carry
        lax.fori_loop(0, 16, narrow, 0)

    same = (lane((16, 256)) % 16) == lax.broadcasted_iota(jnp.int32, (16, 256), 0)
    at = lane((16, 128))
    for h in range(2):
        for g in range(8):
            rows = picked_ref[8 * h + g, pl.ds(pl.multiple_of(8 * step, 8), 8)]
            turned = jnp.concatenate([-rows[:, 128:], rows[:, :128]], axis=1)
            for i in range(8):
                q = (i + g) % 8
                for p, values in ((0, rows), (1, turned)):
                    wide = jnp.where(same, jnp.broadcast_to(values[i:i + 1], (16, 256)), 0.0)
                    weight_ref[g, 128 * p + 16 * q:128 * p + 16 * q + 16] = wide.astype(jnp.bfloat16)
            prod_ref[g] = lax.dot_general(left_ref[8 * h + g], weight_ref[g], NT, preferred_element_type=jnp.float32)

        def place(c, carry):
            rows = pl.ds(pl.multiple_of(16 * c, 16), 16)
            for p in range(2):
                arrays = diagonals([prod_ref[g, rows, 128 * p:128 * p + 128] for g in range(8)], at)
                for i in range(8):
                    x = arrays[-i % 8]
                    x = pltpu.roll(x, (-16 * i) % 128, 1) if i else x
                    out_ref[p, i, rows, 128 * h:128 * h + 128] = x.astype(jnp.bfloat16)
            return carry
        lax.fori_loop(0, chans // 16, place, 0)


def whole(memory_space=pltpu.VMEM):
    return pl.BlockSpec(memory_space=memory_space)


def shards(records, offsets, sources):
    first, second = step_tables()
    coarse, fine = window_tables()
    columns = jnp.concatenate([sources, jnp.full((128 - NSRC,), -1, jnp.int32)])[:, None]
    blocks = pl.pallas_call(
        pack_kernel,
        out_shape=jax.ShapeDtypeStruct((DEVICES, 56, 128), jnp.bfloat16),
        in_specs=[whole(), whole()],
        out_specs=whole(),
        scratch_shapes=[pltpu.VMEM((8, THIRD, 128), jnp.float32), pltpu.VMEM((8, 8, 128), jnp.float32)],
        compiler_params=pltpu.CompilerParams(vmem_limit_bytes=VMEM),
        name="pack",
    )(columns, records)
    received = lax.all_to_all(blocks, ("chan", "freq"), split_axis=0, concat_axis=0, tiled=True)
    white = pl.pallas_call(
        spectrum_kernel,
        out_shape=jax.ShapeDtypeStruct((BANDS, 2, LANES, WIDTH), jnp.bfloat16),
        in_specs=[whole(pltpu.SMEM), whole(pltpu.SMEM)] + [whole()] * 5,
        out_specs=whole(),
        scratch_shapes=[
            pltpu.VMEM((ROWS * DEVICES, 128), jnp.float32),
            pltpu.VMEM((256, LANES), jnp.bfloat16),
            pltpu.VMEM((16, 256, LANES), jnp.bfloat16),
            pltpu.VMEM((2, NF, LANES), jnp.float32),
            pltpu.VMEM((NF + 128, LANES), jnp.bfloat16),
        ],
        compiler_params=pltpu.CompilerParams(vmem_limit_bytes=VMEM),
        name="spectrum",
    )(offsets, fine, received, first, second, band_block(), coarse)
    bands = lax.all_to_all(white, "freq", split_axis=0, concat_axis=0, tiled=True)
    chans = BANDS * OWN
    return pl.pallas_call(
        cross_kernel,
        out_shape=jax.ShapeDtypeStruct((2, NSRC, chans, WIDTH), jnp.bfloat16),
        grid=(NSRC // 8,),
        in_specs=[whole()],
        out_specs=pl.BlockSpec((2, 8, chans, WIDTH), lambda s: (0, s, 0, 0)),
        scratch_shapes=[
            pltpu.VMEM((16, chans, 256), jnp.float32),
            pltpu.VMEM((16, chans, 256), jnp.bfloat16),
            pltpu.VMEM((16, NSRC, 256), jnp.float32),
            pltpu.VMEM((8, 256, 256), jnp.bfloat16),
            pltpu.VMEM((8, chans, 256), jnp.float32),
        ],
        compiler_params=pltpu.CompilerParams(vmem_limit_bytes=VMEM),
        name="cross",
    )(bands)


def solution(mesh):
    in_specs = (P(("chan", "freq"), None), P(), P())
    out_specs = P(None, None, "chan", "freq")
    return jax.shard_map(shards, mesh=mesh, in_specs=in_specs, out_specs=out_specs, check_vma=False)
```

time: 628 us -> 165 us (0.26)
  other arithmetic: 199 us -> 0 us
  local copies, waits for them, and re-layouts: 167 us -> 1.39 us
  waiting for transfers between devices: 150 us -> 0 us
  Pallas kernels: 0 us -> 82.6 us
  blocking collectives: 0 us -> 81 us
  matrix products: 63.6 us -> 0 us
  between operations: 28.4 us -> 0.01 us
  starting transfers between devices: 17.6 us -> 0 us
    another operation x4 -> x0, other arithmetic: 176 us -> none
    psum x1 -> x0, waiting for transfers between devices: 111 us -> none  [shards(): lax.psum(picked.astype(jnp.bfloat16), 'chan').astype(jnp.float32)]
    dot_general x4 -> x0, local copies, waits for them, and re-layouts: 93.2 us -> none  [the longest x1 23.3 us: shards(): jnp.einsum('ksf,krf->srf', source_imag, white_imag)]
    pallas_call x0 -> x3, Pallas kernels: none -> 82.6 us  [the longest x1 43.4 us: shards(): pl.pallas_call(cross_kernel, out_shape=jax.ShapeDtypeStruct((2, NSRC, cha...]
    all_to_all x0 -> x2, blocking collectives: none -> 81 us  [the longest x1 43 us: shards(): lax.all_to_all(white, 'freq', split_axis=0, concat_axis=0, tiled=True)]
    dot_general x7 -> x0, matrix products: 63.6 us -> none  [the longest x1 15.6 us: shards(): jnp.einsum('stc,tf->scf', tapered, table, preferred_element_type=jnp.floa...]
    all_to_all x2 -> x0, waiting for transfers between devices: 38.5 us -> none  [the longest x1 38.5 us: shards(): lax.all_to_all(whitened, 'freq', split_axis=3, concat_axis=1, tiled=True)]
    unnamed x20 -> x0, local copies, waits for them, and re-layouts: 37.8 us -> none
  transfers between devices with their start and end apart: 3 -> 0, of which waited for: 2 -> 0; matrix products, arithmetic and copies ran while one was open for 23% -> 0% of each run, Pallas kernels for 0% -> 0%
where the time goes in v1:
time: 165 us
  Pallas kernels  82.6 us (50%)
  blocking collectives  81 us (49%)
    pallas_call x1, Pallas kernels, shards(): pl.pallas_call(cross_kernel, out_shape=jax.ShapeDtypeStruct((2, NSRC, cha...  43.4 us
    all_to_all x1, blocking collectives, shards(): lax.all_to_all(white, 'freq', split_axis=0, concat_axis=0, tiled=True)  43 us
    all_to_all x1, blocking collectives, shards(): lax.all_to_all(blocks, ('chan', 'freq'), split_axis=0, concat_axis=0, til...  38 us
    pallas_call x1, Pallas kernels, shards(): pl.pallas_call(spectrum_kernel, out_shape=jax.ShapeDtypeStruct((BANDS, 2,...  33.6 us
    pallas_call x1, Pallas kernels, shards(): pl.pallas_call(pack_kernel, out_shape=jax.ShapeDtypeStruct((DEVICES, 56,...  5.57 us

profile of v1, /device:TPU:0, one launch (start us, length us, event | category | flops | bytes accessed | tf_op | source)
XLA Modules:
  0.0 165.0 jit_solution(7795074991612981385)
XLA Ops:
  0.0 0.7 pad_bitcast_fusion
  0.7 0.7 copy.9.sources_ref
  1.4 5.6 %pack.1 = bf16[128,56,128]{2,1,0:T(8,128)(2,1)} custom-call(s32[128,1]{1,0:T(8,128)} %copy.9.sources_ref, bf16[144,5120]{1,0:T(8,128)(2,1)} %records_ref.1), custom_call_target="tpu_custom_call" | custom-call | tf_op jit(solution)/shard_map/pack/pallas_call | solution.py:275
  7.0 38.0 %all_to_all.10.got_ref = bf16[128,56,128]{2,1,0:T(8,128)(2,1)} all-to-all(bf16[128,56,128]{2,1,0:T(8,128)(2,1)} %pack.1), channel_id=1, replica_groups=mesh['chan'=16,'freq'=8] {'chan','freq'}, dimensions={0} | all-to-all | bytes 3670016 | tf_op jit(solution)/shard_map/all_to_all | solution.py:284
  44.9 33.6 %spectrum.1 = bf16[8,2,384,256]{3,2,1,0:T(8,128)(2,1)} custom-call(s32[8]{0:T(128)} %offsets_ref.1, f32[2,16]{1,0:T(2,128)} %constant.12.clone.fine_ref, bf16[128,56,128]{2,1,0:T(8,128)(2,1)} %all_to_all.10.got_ref, bf16[256,256]{1,0:T(8,128)(2,1)} %constant.13.clone.first_ref, bf16[16,256,256]{2,1,0:T(8,128)(2,1)} %constant.14.clone.second_ref, ...), custom_call_target="tpu_custom_call" | custom-call | tf_op jit(solution)/shard_map/spectrum/pallas_call | solution.py:285
  78.5 43.0 %all_to_all.11.got_ref = bf16[8,2,384,256]{3,2,1,0:T(8,128)(2,1)} all-to-all(bf16[8,2,384,256]{3,2,1,0:T(8,128)(2,1)} %spectrum.1), channel_id=1, replica_groups=mesh['chan'=16,'freq'=8] {'freq'}, dimensions={0} | all-to-all | bytes 6291456 | tf_op jit(solution)/shard_map/all_to_all | solution.py:300
  121.6 43.4 %cross.1 = bf16[2,64,320,256]{3,2,1,0:T(8,128)(2,1)} custom-call(bf16[8,2,384,256]{3,2,1,0:T(8,128)(2,1)} %all_to_all.11.got_ref), custom_call_target="tpu_custom_call" | custom-call | tf_op jit(solution)/shard_map/cross/pallas_call | solution.py:302

commit v2 on v1

--- a/solution.py
+++ b/solution.py
@@ -87,11 +87,12 @@
 
 
 def pack_kernel(sources_ref, records_ref, out_ref, head_ref, tail_ref):
-    picked = jnp.zeros((ROWS, 128), jnp.float32)
+    picked = jnp.zeros((ROWS, NSRC), jnp.float32)
     for i in range(8):
-        cols = lane((128, 640)) + 640 * i
-        hot = (cols == sources_ref[...]).astype(jnp.bfloat16)
-        picked += lax.dot_general(records_ref[:, 640 * i:640 * i + 640], hot, NT, preferred_element_type=jnp.float32)
+        rows = lax.broadcasted_iota(jnp.int32, (640, NSRC), 0) + 640 * i
+        hot = (rows == sources_ref[...]).astype(jnp.bfloat16)
+        picked += jnp.dot(records_ref[:, 640 * i:640 * i + 640], hot, preferred_element_type=jnp.float32)
+    picked = jnp.concatenate([picked, jnp.zeros((ROWS, 128 - NSRC), jnp.float32)], axis=1)
     at8 = lane((8, 128))
     for band in range(BANDS):
         head_ref[band] = pltpu.roll(picked[:THIRD], (120 - 8 * band) % 128, 1)
@@ -133,36 +134,42 @@
         by48 = pltpu.roll(main, 48, 1)
         by88 = pltpu.roll(main, 88, 1)
         tails = [pltpu.roll(tail, (OWN - 8 * m) % 128, 1) for m in range(12)]
-        base = pl.multiple_of(src * ROWS, 8)
-        time_ref[pl.ds(base, THIRD)] = jnp.where(own48, main, by48)
-        time_ref[pl.ds(base + THIRD, THIRD)] = jnp.where(own48, by88, jnp.concatenate(tails[:6], axis=0))
-        time_ref[pl.ds(base + 2 * THIRD, THIRD)] = jnp.where(own48, by48, jnp.concatenate(tails[6:], axis=0))
-        return carry
-    lax.fori_loop(0, DEVICES, unpack, 0)
+        thirds = [
+            jnp.where(own48, main, by48),
+            jnp.where(own48, by88, jnp.concatenate(tails[:6], axis=0)),
+            jnp.where(own48, by48, jnp.concatenate(tails[6:], axis=0)),
+        ]
+        for i in range(9):
+            time_ref[pl.ds(src * 153 + 17 * i, 16)] = thirds[i // 3][16 * (i % 3):16 * (i % 3) + 16]
+        return carry
+    lax.fori_loop(0, DEVICES, unpack, 0, unroll=8)
 
     at = lane((64, 128))
 
-    def residue(b, carry):
-        cb, sb = fine_ref[0, b], fine_ref[1, b]
-        for chunk in range(4):
-            rows = slice(64 * chunk, 64 * chunk + 64)
-            window = 0.5 - 0.5 * (coarse_ref[0, rows] * cb - coarse_ref[1, rows] * sb)
-            placed = []
-            for k in range(SEG):
-                start = offsets_ref[k] + b + 1024 * chunk
-                piece = time_ref[pl.ds(start, 64, 16)] * window
-                shift = (CHANS * k) % 128
-                placed.append(pltpu.roll(piece, shift, 1) if shift else piece)
-            t0 = jnp.where(at < 48, placed[0], jnp.where(at < 96, placed[1], placed[2]))
-            t1 = jnp.where(at < 16, placed[2], jnp.where(at < 64, placed[3], jnp.where(at < 112, placed[4], placed[5])))
-            t2 = jnp.where(at < 32, placed[5], jnp.where(at < 80, placed[6], placed[7]))
-            x_ref[rows] = jnp.concatenate([t0, t1, t2], axis=1).astype(jnp.bfloat16)
-        y = jnp.dot(first_ref[...], x_ref[...], preferred_element_type=jnp.float32).astype(jnp.bfloat16)
-        base = pl.multiple_of(16 * b, 16)
-        for g in range(16):
-            y_ref[g, pl.ds(base, 16)] = y[16 * g:16 * g + 16]
-        return carry
-    lax.fori_loop(0, 16, residue, 0)
+    def residues(quad, carry):
+        for j in range(4):
+            b = 4 * quad + j
+            cb, sb = fine_ref[0, b], fine_ref[1, b]
+            starts = [offsets_ref[k] + b for k in range(SEG)]
+            starts = [start + lax.shift_right_logical(start, 4) for start in starts]
+            for chunk in range(4):
+                rows = slice(64 * chunk, 64 * chunk + 64)
+                window = 0.5 - 0.5 * (coarse_ref[0, rows] * cb - coarse_ref[1, rows] * sb)
+                placed = []
+                for k in range(SEG):
+                    piece = time_ref[pl.ds(starts[k] + 17 * 64 * chunk, 64, 17)] * window
+                    shift = (CHANS * k) % 128
+                    placed.append(pltpu.roll(piece, shift, 1) if shift else piece)
+                t0 = jnp.where(at < 48, placed[0], jnp.where(at < 96, placed[1], placed[2]))
+                t1 = jnp.where(at < 16, placed[2], jnp.where(at < 64, placed[3], jnp.where(at < 112, placed[4], placed[5])))
+                t2 = jnp.where(at < 32, placed[5], jnp.where(at < 80, placed[6], placed[7]))
+                x_ref[j, rows] = jnp.concatenate([t0, t1, t2], axis=1).astype(jnp.bfloat16)
+            y = jnp.dot(first_ref[...], x_ref[j], preferred_element_type=jnp.float32).astype(jnp.bfloat16)
+            base = pl.multiple_of(16 * b, 16)
+            for g in range(16):
+                y_ref[g, pl.ds(base, 16)] = y[16 * g:16 * g + 16]
+        return carry
+    lax.fori_loop(0, 4, residues, 0)
 
     for g in range(16):
         z = jnp.dot(second_ref[g], y_ref[g], preferred_element_type=jnp.float32)
@@ -185,7 +192,7 @@
         re, im = spec_ref[0, rows], spec_ref[1, rows]
         mag_ref[pl.ds(pl.multiple_of(i * 64 + 64, 64), 64)] = jnp.sqrt(re * re + im * im).astype(jnp.bfloat16)
         return carry
-    lax.fori_loop(0, NF // 64, magnitude, 0)
+    lax.fori_loop(0, NF // 64, magnitude, 0, unroll=4)
 
     def whiten(band, carry):
         for half in range(2):
@@ -200,7 +207,7 @@
                     turned = jnp.transpose(white[:, 128 * t:128 * t + 128])
                     out_ref[band, p, 128 * t:128 * t + 128, 128 * half:128 * half + 128] = turned.astype(jnp.bfloat16)
         return carry
-    lax.fori_loop(0, BANDS, whiten, 0)
+    lax.fori_loop(0, BANDS, whiten, 0, unroll=4)
 
 
 def diagonals(arrays, at):
@@ -237,31 +244,36 @@
         def narrow(g, carry):
             left_ref[g] = wide_ref[g].astype(jnp.bfloat16)
             return carry
-        lax.fori_loop(0, 16, narrow, 0)
+        lax.fori_loop(0, 16, narrow, 0, unroll=4)
 
     same = (lane((16, 256)) % 16) == lax.broadcasted_iota(jnp.int32, (16, 256), 0)
     at = lane((16, 128))
+
+    def multiply(h, g):
+        rows = picked_ref[8 * h + g, pl.ds(pl.multiple_of(8 * step, 8), 8)]
+        turned = jnp.concatenate([-rows[:, 128:], rows[:, :128]], axis=1)
+        for i in range(8):
+            q = (i + g) % 8
+            for p, values in ((0, rows), (1, turned)):
+                wide = jnp.where(same, jnp.broadcast_to(values[i:i + 1], (16, 256)), 0.0)
+                weight_ref[h, g, 128 * p + 16 * q:128 * p + 16 * q + 16] = wide.astype(jnp.bfloat16)
+        prod = lax.dot_general(left_ref[8 * h + g], weight_ref[h, g], NT, preferred_element_type=jnp.float32)
+        prod_ref[h, g] = prod.astype(jnp.bfloat16)
+
+    def place(h, c):
+        rows = slice(16 * c, 16 * c + 16)
+        for p in range(2):
+            arrays = diagonals([prod_ref[h, g, rows, 128 * p:128 * p + 128] for g in range(8)], at)
+            for i in range(8):
+                x = arrays[-i % 8]
+                x = pltpu.roll(x, (-16 * i) % 128, 1) if i else x
+                out_ref[p, i, rows, 128 * h:128 * h + 128] = x
+
     for h in range(2):
         for g in range(8):
-            rows = picked_ref[8 * h + g, pl.ds(pl.multiple_of(8 * step, 8), 8)]
-            turned = jnp.concatenate([-rows[:, 128:], rows[:, :128]], axis=1)
-            for i in range(8):
-                q = (i + g) % 8
-                for p, values in ((0, rows), (1, turned)):
-                    wide = jnp.where(same, jnp.broadcast_to(values[i:i + 1], (16, 256)), 0.0)
-                    weight_ref[g, 128 * p + 16 * q:128 * p + 16 * q + 16] = wide.astype(jnp.bfloat16)
-            prod_ref[g] = lax.dot_general(left_ref[8 * h + g], weight_ref[g], NT, preferred_element_type=jnp.float32)
-
-        def place(c, carry):
-            rows = pl.ds(pl.multiple_of(16 * c, 16), 16)
-            for p in range(2):
-                arrays = diagonals([prod_ref[g, rows, 128 * p:128 * p + 128] for g in range(8)], at)
-                for i in range(8):
-                    x = arrays[-i % 8]
-                    x = pltpu.roll(x, (-16 * i) % 128, 1) if i else x
-                    out_ref[p, i, rows, 128 * h:128 * h + 128] = x.astype(jnp.bfloat16)
-            return carry
-        lax.fori_loop(0, chans // 16, place, 0)
+            multiply(h, g)
+        for c in range(chans // 16):
+            place(h, c)
 
 
 def whole(memory_space=pltpu.VMEM):
@@ -271,7 +283,6 @@
 def shards(records, offsets, sources):
     first, second = step_tables()
     coarse, fine = window_tables()
-    columns = jnp.concatenate([sources, jnp.full((128 - NSRC,), -1, jnp.int32)])[:, None]
     blocks = pl.pallas_call(
         pack_kernel,
         out_shape=jax.ShapeDtypeStruct((DEVICES, 56, 128), jnp.bfloat16),
@@ -280,7 +291,7 @@
         scratch_shapes=[pltpu.VMEM((8, THIRD, 128), jnp.float32), pltpu.VMEM((8, 8, 128), jnp.float32)],
         compiler_params=pltpu.CompilerParams(vmem_limit_bytes=VMEM),
         name="pack",
-    )(columns, records)
+    )(sources[None, :], records)
     received = lax.all_to_all(blocks, ("chan", "freq"), split_axis=0, concat_axis=0, tiled=True)
     white = pl.pallas_call(
         spectrum_kernel,
@@ -288,8 +299,8 @@
         in_specs=[whole(pltpu.SMEM), whole(pltpu.SMEM)] + [whole()] * 5,
         out_specs=whole(),
         scratch_shapes=[
-            pltpu.VMEM((ROWS * DEVICES, 128), jnp.float32),
-            pltpu.VMEM((256, LANES), jnp.bfloat16),
+            pltpu.VMEM((ROWS * DEVICES // 16 * 17, 128), jnp.float32),
+            pltpu.VMEM((4, 256, LANES), jnp.bfloat16),
             pltpu.VMEM((16, 256, LANES), jnp.bfloat16),
             pltpu.VMEM((2, NF, LANES), jnp.float32),
             pltpu.VMEM((NF + 128, LANES), jnp.bfloat16),
@@ -309,8 +320,8 @@
             pltpu.VMEM((16, chans, 256), jnp.float32),
             pltpu.VMEM((16, chans, 256), jnp.bfloat16),
             pltpu.VMEM((16, NSRC, 256), jnp.float32),
-            pltpu.VMEM((8, 256, 256), jnp.bfloat16),
-            pltpu.VMEM((8, chans, 256), jnp.float32),
+            pltpu.VMEM((2, 8, 256, 256), jnp.bfloat16),
+            pltpu.VMEM((2, 8, chans, 256), jnp.bfloat16),
         ],
         compiler_params=pltpu.CompilerParams(vmem_limit_bytes=VMEM),
         name="cross",

time: 165 us -> 119 us (0.72)
  Pallas kernels: 82.6 us -> 38 us
    pallas_call x1, Pallas kernels: 43.4 us -> 17.5 us  [shards(): pl.pallas_call(cross_kernel, out_shape=jax.ShapeDtypeStruct((2, NSRC, cha...]
    pallas_call x1, Pallas kernels: 33.6 us -> 15 us  [shards(): pl.pallas_call(spectrum_kernel, out_shape=jax.ShapeDtypeStruct((BANDS, 2,...]
where the time goes in v2:
time: 119 us
  blocking collectives  81 us (68%)
  Pallas kernels  38 us (32%)
    all_to_all x1, blocking collectives, shards(): lax.all_to_all(white, 'freq', split_axis=0, concat_axis=0, tiled=True)  43 us
    all_to_all x1, blocking collectives, shards(): lax.all_to_all(blocks, ('chan', 'freq'), split_axis=0, concat_axis=0, til...  38 us
    pallas_call x1, Pallas kernels, shards(): pl.pallas_call(cross_kernel, out_shape=jax.ShapeDtypeStruct((2, NSRC, cha...  17.5 us
    pallas_call x1, Pallas kernels, shards(): pl.pallas_call(spectrum_kernel, out_shape=jax.ShapeDtypeStruct((BANDS, 2,...  15 us
    pallas_call x1, Pallas kernels, shards(): pl.pallas_call(pack_kernel, out_shape=jax.ShapeDtypeStruct((DEVICES, 56,...  5.49 us

profile of v2, /device:TPU:0, one launch (start us, length us, event | category | flops | bytes accessed | tf_op | source)
XLA Modules:
  0.0 119.0 jit_solution(17885912459958900909)
XLA Ops:
  0.0 5.5 %pack.1 = bf16[128,56,128]{2,1,0:T(8,128)(2,1)} custom-call(s32[1,64]{1,0:T(1,128)} %bitcast.1, bf16[144,5120]{1,0:T(8,128)(2,1)} %records_ref.1), custom_call_target="tpu_custom_call" | custom-call | tf_op jit(solution)/shard_map/pack/pallas_call | solution.py:286
  5.5 38.0 %all_to_all.10.got_ref = bf16[128,56,128]{2,1,0:T(8,128)(2,1)} all-to-all(bf16[128,56,128]{2,1,0:T(8,128)(2,1)} %pack.1), channel_id=1, replica_groups=mesh['chan'=16,'freq'=8] {'chan','freq'}, dimensions={0} | all-to-all | bytes 3670016 | tf_op jit(solution)/shard_map/all_to_all | solution.py:295
  43.5 15.0 %spectrum.1 = bf16[8,2,384,256]{3,2,1,0:T(8,128)(2,1)} custom-call(s32[8]{0:T(128)} %offsets_ref.1, f32[2,16]{1,0:T(2,128)} %constant.10.clone.fine_ref, bf16[128,56,128]{2,1,0:T(8,128)(2,1)} %all_to_all.10.got_ref, bf16[256,256]{1,0:T(8,128)(2,1)} %constant.11.clone.first_ref, bf16[16,256,256]{2,1,0:T(8,128)(2,1)} %constant.12.clone.second_ref, ...), custom_call_target="tpu_custom_call" | custom-call | tf_op jit(solution)/shard_map/spectrum/pallas_call | solution.py:296
  58.4 43.0 %all_to_all.11.got_ref = bf16[8,2,384,256]{3,2,1,0:T(8,128)(2,1)} all-to-all(bf16[8,2,384,256]{3,2,1,0:T(8,128)(2,1)} %spectrum.1), channel_id=1, replica_groups=mesh['chan'=16,'freq'=8] {'freq'}, dimensions={0} | all-to-all | bytes 6291456 | tf_op jit(solution)/shard_map/all_to_all | solution.py:311
  101.5 17.5 %cross.1 = bf16[2,64,320,256]{3,2,1,0:T(8,128)(2,1)} custom-call(bf16[8,2,384,256]{3,2,1,0:T(8,128)(2,1)} %all_to_all.11.got_ref), custom_call_target="tpu_custom_call" | custom-call | tf_op jit(solution)/shard_map/cross/pallas_call | solution.py:313
